TPU v7x, 32 devices: a whole 2x2x4 slice. The times are simulated.
32 devices in a mesh: row: 4 (over x, core), col: 8 (over z, y).
Axes of the slice: x: 2, y: 2, z: 4, core: 2. Of those that a mesh axis runs over, the one named last changes fastest.
Arguments:
- matrix: float32 [8192, 4096], P('row', 'col'), may hold values from 0 to 2, as said below
Outputs:
- factored: float32 [8192, 4096], P('row', 'col')
Inputs may be any that keep to these rules, and one draw needn't show every extreme that they name: In grid order, the matrix is the leading 4096 columns of a symmetric positive definite matrix of order 8192.
All inputs are finite; a program needn't handle non-finite values.
Results may differ from a plain program's by a relative error of at most 0.0011.
Values may be sent and summed in bfloat16 or wider, within the bound.
A program may use at most 64 MiB of HBM per device.

v0:
```python
import jax
import jax.numpy as jnp
from jax import lax
from jax.sharding import PartitionSpec as P

TILE = 256
PANELS = 3


def broadcast(value, axis, source):
    kept = jnp.where(lax.axis_index(axis) == source, value, 0).astype(value.dtype)
    return lax.psum(kept, axis)


def factor_tile(square):
    factor = jnp.linalg.cholesky(square)
    eye_tile = jnp.eye(square.shape[0], dtype=square.dtype)
    inverse = jax.scipy.linalg.solve_triangular(factor, eye_tile, lower=True)
    return (factor, inverse)


def tile_product(left_rows, right_rows):
    return lax.dot_general(
        left_rows, right_rows, (((1,), (1,)), ((), ())), preferred_element_type=jnp.float32
    )


def on_device(matrix):
    row_count = lax.axis_size("row")
    col_count = lax.axis_size("col")
    row_index = lax.axis_index("row")
    col_index = lax.axis_index("col")
    tiles_down = matrix.shape[0] // TILE
    tiles_across = matrix.shape[1] // TILE
    row_global = jnp.repeat(jnp.arange(tiles_down, dtype=jnp.int32) * row_count + row_index, TILE)
    col_global = jnp.repeat(jnp.arange(tiles_across, dtype=jnp.int32) * col_count + col_index, TILE)
    source_row = col_index % row_count
    chosen_index = (col_index + col_count * jnp.arange(tiles_across, dtype=jnp.int32)) // row_count
    blocks = matrix
    for panel_step in range(PANELS):
        diag_row = panel_step % row_count
        diag_down = panel_step // row_count
        owner_col = panel_step % col_count
        owner_across = panel_step // col_count
        diagonal_block = blocks[
            diag_down * TILE : (diag_down + 1) * TILE,
            owner_across * TILE : (owner_across + 1) * TILE,
        ]
        factor, inverse = factor_tile(diagonal_block)
        factor, inverse = (broadcast(factor, "row", diag_row), broadcast(inverse, "row", diag_row))
        column_old = blocks[:, owner_across * TILE : (owner_across + 1) * TILE]
        solved = jnp.dot(
            column_old,
            inverse.T,
            precision=lax.Precision.HIGHEST,
            preferred_element_type=jnp.float32,
        )
        below_step = (row_global > panel_step)[:, None]
        solved = jnp.where(below_step, solved, jnp.float32(0.0))
        factor_rows = broadcast(solved.astype(jnp.bfloat16), "col", owner_col)
        chosen = factor_rows.reshape(tiles_down, TILE, TILE)[chosen_index].reshape(
            tiles_across * TILE, TILE
        )
        across_rows = broadcast(chosen, "row", source_row)
        keep_tile = jnp.logical_and(
            row_global[:, None] >= col_global[None, :], (col_global > panel_step)[None, :]
        )
        product = tile_product(factor_rows, across_rows)
        updated = blocks - jnp.where(keep_tile, product, jnp.float32(0.0))
        factor_stack = jnp.tile(factor, (tiles_down, 1))
        new_column = jnp.where((row_global == panel_step)[:, None], factor_stack, column_old)
        new_column = jnp.where(below_step, solved, new_column)
        column_now = jnp.where(
            col_index == owner_col,
            new_column,
            updated[:, owner_across * TILE : (owner_across + 1) * TILE],
        )
        blocks = updated.at[:, owner_across * TILE : (owner_across + 1) * TILE].set(column_now)
    return blocks


def solution(mesh):
    in_specs = (P("row", "col"),)
    out_specs = P("row", "col")
    return jax.shard_map(
        on_device, mesh=mesh, in_specs=in_specs, out_specs=out_specs, check_vma=False
    )
```

profile of v0, /device:TPU:26, one launch (start us, length us, event | category | flops | bytes accessed | tf_op | source)
XLA Modules:
  0.0 696.4 jit_solution(1444956091003030889)
XLA Ops:
  6.6 5.3 copy.22
  11.9 1.0 slice.143
  13.0 1.0 fusion.5
  14.0 11.7 %cholesky.172 = f32[128,128]{1,0:T(8,128)S(1)} custom-call(f32[128,128]{1,0:T(8,128)S(1)} %cholesky.270), custom_call_target="Cholesky" | custom-call | tf_op jit(solution)/shard_map/jit(cholesky)/cholesky | solution.py:16
  25.8 9.8 %custom-call.15 = f32[1,128,128]{1,2,0:T(8,128)S(1)} custom-call(f32[1,128,128]{2,1,0:T(8,128)S(1)} %get-tuple-element.123), custom_call_target="InvertDiagBlocksLowerTriangular" | custom-call | tf_op jit(solution)/shard_map/jit(cholesky)/cholesky | solution.py:16
  36.1 11.7 %cholesky.189 = f32[128,128]{1,0:T(8,128)S(1)} custom-call(f32[128,128]{1,0:T(8,128)S(1)} %convolution_subtract_fusion.5), custom_call_target="Cholesky" | custom-call | tf_op jit(solution)/shard_map/jit(cholesky)/cholesky | solution.py:16
  47.8 0.7 compare_reduce_fusion.4
  49.9 0.7 fusion.11
  50.7 4.1 while.9
  51.4 1.4 bitcast_dynamic-update-slice_fusion.6
  53.4 1.4 bitcast_dynamic-update-slice_fusion.6
  54.8 19.9 %custom-call.16 = f32[2,128,128]{1,2,0:T(8,128)S(1)} custom-call(f32[2,128,128]{2,1,0:T(8,128)S(1)} %get-tuple-element.63), custom_call_target="InvertDiagBlocksLowerTriangular" | custom-call | tf_op jit(solution)/shard_map/jit(_solve_triangular)/triangular_solve | solution.py:18
  75.6 0.7 maximum_select_fusion
  76.5 33.4 %all-reduce.30.cloned.1.call-done = (f32[256,256]{1,0:T(8,128)}, f32[256,256]{1,0:T(8,128)}) async-done(((f32[256,256]{1,0:T(8,128)}, f32[256,256]{1,0:T(8,128)}), (f32[256,256]{1,0:T(8,128)}, f32[256,256]{1,0:T(8,128)})) %all-reduce.30.cloned.1.call-update) | async-done | bytes 524304 | tf_op jit(solution)/shard_map/psum | solution.py:12
  109.9 5.3 convert_select_fusion.2
  116.0 77.2 %all-reduce.14.cloned.1.call-done = bf16[2048,256]{0,1:T(8,128)(2,1)} async-done(((bf16[2048,256]{0,1:T(8,128)(2,1)}), bf16[2048,256]{0,1:T(8,128)(2,1)}) %all-reduce.14.cloned.1.call-update) | async-done | bytes 1048592 | tf_op jit(solution)/shard_map/psum | solution.py:12
  193.2 1.5 copy.40
  195.2 0.7 broadcast_select_fusion.2
  196.4 2.2 copy.45
  198.6 29.2 %all-reduce.16.cloned.1.call-done = bf16[512,256]{1,0:T(8,128)(2,1)} async-done(((bf16[512,256]{1,0:T(8,128)(2,1)}), bf16[512,256]{1,0:T(8,128)(2,1)}) %all-reduce.16.cloned.1.call-update) | async-done | bytes 262160 | tf_op jit(solution)/shard_map/psum | solution.py:12
  227.8 3.5 select_subtract_fusion.2
  232.6 1.9 constant_dynamic-update-slice_fusion.7
  234.5 2.0 copy-done.1
  236.7 11.7 %cholesky.206 = f32[128,128]{1,0:T(8,128)S(1)} custom-call(f32[128,128]{1,0:T(8,128)S(1)} %cholesky.273), custom_call_target="Cholesky" | custom-call | tf_op jit(solution)/shard_map/jit(cholesky)/cholesky | solution.py:16
  248.5 9.8 %custom-call.17 = f32[1,128,128]{1,2,0:T(8,128)S(1)} custom-call(f32[1,128,128]{2,1,0:T(8,128)S(1)} %get-tuple-element.119), custom_call_target="InvertDiagBlocksLowerTriangular" | custom-call | tf_op jit(solution)/shard_map/jit(cholesky)/cholesky | solution.py:16
  258.8 12.1 %cholesky.223 = f32[128,128]{1,0:T(8,128)S(1)} custom-call(f32[128,128]{1,0:T(8,128)S(1)} %convolution_subtract_fusion.4), custom_call_target="Cholesky" | custom-call | tf_op jit(solution)/shard_map/jit(cholesky)/cholesky | solution.py:16
  270.9 0.7 compare_reduce_fusion.2
  271.6 0.7 compare_reduce_fusion.3
  273.6 0.7 fusion.12
  274.3 4.1 while.10
  275.0 1.4 bitcast_dynamic-update-slice_fusion.7
  277.1 1.4 bitcast_dynamic-update-slice_fusion.7
  278.5 19.7 %custom-call.18 = f32[2,128,128]{1,2,0:T(8,128)S(1)} custom-call(f32[2,128,128]{2,1,0:T(8,128)S(1)} %get-tuple-element.64), custom_call_target="InvertDiagBlocksLowerTriangular" | custom-call | tf_op jit(solution)/shard_map/jit(_solve_triangular)/triangular_solve | solution.py:18
  299.1 0.7 maximum_select_fusion.1
  299.9 33.6 %all-reduce.28.cloned.1.call-done = (f32[256,256]{1,0:T(8,128)}, f32[256,256]{1,0:T(8,128)}) async-done(((f32[256,256]{1,0:T(8,128)}, f32[256,256]{1,0:T(8,128)}), (f32[256,256]{1,0:T(8,128)}, f32[256,256]{1,0:T(8,128)})) %all-reduce.28.cloned.1.call-update) | async-done | bytes 524304 | tf_op jit(solution)/shard_map/psum | solution.py:12
  333.5 4.7 convert_select_fusion.1
  338.3 77.9 %all-reduce.18.cloned.1.call-done = bf16[2048,256]{0,1:T(8,128)(2,1)} async-done(((bf16[2048,256]{0,1:T(8,128)(2,1)}), bf16[2048,256]{0,1:T(8,128)(2,1)}) %all-reduce.18.cloned.1.call-update) | async-done | bytes 1048592 | tf_op jit(solution)/shard_map/psum | solution.py:12
  416.1 1.5 copy.41
  418.2 0.7 broadcast_select_fusion.1
  419.5 2.2 copy.46
  421.7 29.0 %all-reduce.20.cloned.1.call-done = bf16[512,256]{1,0:T(8,128)(2,1)} async-done(((bf16[512,256]{1,0:T(8,128)(2,1)}), bf16[512,256]{1,0:T(8,128)(2,1)}) %all-reduce.20.cloned.1.call-update) | async-done | bytes 262160 | tf_op jit(solution)/shard_map/psum | solution.py:12
  450.7 5.5 select_subtract_fusion.1
  456.3 4.3 constant_dynamic-update-slice_fusion.6
  460.8 11.7 %cholesky.240 = f32[128,128]{1,0:T(8,128)S(1)} custom-call(f32[128,128]{1,0:T(8,128)S(1)} %cholesky.276), custom_call_target="Cholesky" | custom-call | tf_op jit(solution)/shard_map/jit(cholesky)/cholesky | solution.py:16
  472.6 9.8 %custom-call.19 = f32[1,128,128]{1,2,0:T(8,128)S(1)} custom-call(f32[1,128,128]{2,1,0:T(8,128)S(1)} %get-tuple-element.115), custom_call_target="InvertDiagBlocksLowerTriangular" | custom-call | tf_op jit(solution)/shard_map/jit(cholesky)/cholesky | solution.py:16
  482.9 11.9 %cholesky.257 = f32[128,128]{1,0:T(8,128)S(1)} custom-call(f32[128,128]{1,0:T(8,128)S(1)} %convolution_subtract_fusion.3), custom_call_target="Cholesky" | custom-call | tf_op jit(solution)/shard_map/jit(cholesky)/cholesky | solution.py:16
  494.8 0.7 compare_reduce_fusion
  497.4 0.7 fusion.13
  498.2 4.0 while.11
  498.8 1.3 bitcast_dynamic-update-slice_fusion.8
  500.8 1.3 bitcast_dynamic-update-slice_fusion.8
  502.2 19.7 %custom-call.20 = f32[2,128,128]{1,2,0:T(8,128)S(1)} custom-call(f32[2,128,128]{2,1,0:T(8,128)S(1)} %get-tuple-element.65), custom_call_target="InvertDiagBlocksLowerTriangular" | custom-call | tf_op jit(solution)/shard_map/jit(_solve_triangular)/triangular_solve | solution.py:18
  522.8 0.7 maximum_select_fusion.2
  523.6 33.6 %all-reduce.26.cloned.1.call-done = (f32[256,256]{1,0:T(8,128)}, f32[256,256]{1,0:T(8,128)}) async-done(((f32[256,256]{1,0:T(8,128)}, f32[256,256]{1,0:T(8,128)}), (f32[256,256]{1,0:T(8,128)}, f32[256,256]{1,0:T(8,128)})) %all-reduce.26.cloned.1.call-update) | async-done | bytes 524304 | tf_op jit(solution)/shard_map/psum | solution.py:12
  557.2 4.7 convert_select_fusion
  561.9 77.9 %all-reduce.22.cloned.1.call-done = bf16[2048,256]{0,1:T(8,128)(2,1)} async-done(((bf16[2048,256]{0,1:T(8,128)(2,1)}), bf16[2048,256]{0,1:T(8,128)(2,1)}) %all-reduce.22.cloned.1.call-update) | async-done | bytes 1048592 | tf_op jit(solution)/shard_map/psum | solution.py:12
  639.9 1.5 copy.42
  641.9 0.7 broadcast_select_fusion
  642.7 1.1 copy.33
  643.9 2.2 copy.47
  646.2 28.3 %all-reduce.24.cloned.1.call-done = bf16[512,256]{1,0:T(8,128)(2,1)} async-done(((bf16[512,256]{1,0:T(8,128)(2,1)}), bf16[512,256]{1,0:T(8,128)(2,1)}) %all-reduce.24.cloned.1.call-update) | async-done | bytes 262160 | tf_op jit(solution)/shard_map/psum | solution.py:12
  674.4 5.5 select_subtract_fusion
  679.9 4.4 fusion.1
  684.3 5.3 copy.34
  (119 shorter events, 14.7 us)
Async XLA Ops:
  6.5 103.3 %all-reduce.30.cloned.1.call-start = ((), (), s32[]{:S(2)}) async-start(), calls=%async_computation.8 | async-start | bytes 1048576 | tf_op jit(solution)/shard_map/psum | solution.py:12
  76.3 116.9 %all-reduce.14.cloned.1.call-start = ((), (), s32[]{:S(2)}) async-start(), calls=%async_computation | async-start | bytes 2097152 | tf_op jit(solution)/shard_map/psum | solution.py:12
  115.2 80.9 %copy-start.13 = (f32[256,256]{1,0:T(8,128)S(1)}, f32[256,256]{1,0:T(8,128)}, u32[]{:S(2)}) copy-start(f32[256,256]{1,0:T(8,128)} %get-tuple-element.95) | copy-start | bytes 786436
  115.2 112.5 %all-reduce.16.cloned.1.call-start = ((), (), s32[]{:S(2)}) async-start(), calls=%async_computation.1 | async-start | bytes 524288 | tf_op jit(solution)/shard_map/psum | solution.py:12
  196.0 137.5 %all-reduce.28.cloned.1.call-start = ((), (), s32[]{:S(2)}) async-start(), calls=%async_computation.7 | async-start | bytes 1048576 | tf_op jit(solution)/shard_map/psum | solution.py:12
  196.3 31.4 %copy-start.10 = (bf16[2048,256]{0,1:T(8,128)(2,1)S(1)}, bf16[2048,256]{0,1:T(8,128)(2,1)}, u32[]{:S(2)}) copy-start(bf16[2048,256]{0,1:T(8,128)(2,1)} %all-reduce.14.cloned.1.call-done) | copy-start | bytes 3145732
  227.8 3.6 copy-start
  227.8 4.2 copy-start.6
  227.8 4.8 copy-start.9
  234.4 2.0 copy-start.1
  236.5 97.0 %copy-start.2 = (f32[2048,256]{0,1:T(8,128)}, f32[2048,256]{0,1:T(8,128)S(1)}, u32[]{:S(2)}) copy-start(f32[2048,256]{0,1:T(8,128)S(1)} %get-tuple-element.99) | copy-start | bytes 6291460
  299.8 116.3 %all-reduce.18.cloned.1.call-start = ((), (), s32[]{:S(2)}) async-start(), calls=%async_computation.2 | async-start | bytes 2097152 | tf_op jit(solution)/shard_map/psum | solution.py:12
  338.2 81.0 %copy-start.14 = (f32[256,256]{1,0:T(8,128)S(1)}, f32[256,256]{1,0:T(8,128)}, u32[]{:S(2)}) copy-start(f32[256,256]{1,0:T(8,128)} %get-tuple-element.93) | copy-start | bytes 786436
  338.2 112.5 %all-reduce.20.cloned.1.call-start = ((), (), s32[]{:S(2)}) async-start(), calls=%async_computation.3 | async-start | bytes 524288 | tf_op jit(solution)/shard_map/psum | solution.py:12
  418.9 138.2 %all-reduce.26.cloned.1.call-start = ((), (), s32[]{:S(2)}) async-start(), calls=%async_computation.6 | async-start | bytes 1048576 | tf_op jit(solution)/shard_map/psum | solution.py:12
  419.5 31.2 %copy-start.12 = (bf16[2048,256]{0,1:T(8,128)(2,1)S(1)}, bf16[2048,256]{0,1:T(8,128)(2,1)}, u32[]{:S(2)}) copy-start(bf16[2048,256]{0,1:T(8,128)(2,1)} %all-reduce.18.cloned.1.call-done) | copy-start | bytes 3145732
  450.7 5.6 copy-start.3
  450.7 5.6 copy-start.7
  450.7 5.6 copy-start.8
  523.5 116.3 %all-reduce.22.cloned.1.call-start = ((), (), s32[]{:S(2)}) async-start(), calls=%async_computation.4 | async-start | bytes 2097152 | tf_op jit(solution)/shard_map/psum | solution.py:12
  561.9 112.5 %all-reduce.24.cloned.1.call-start = ((), (), s32[]{:S(2)}) async-start(), calls=%async_computation.5 | async-start | bytes 524288 | tf_op jit(solution)/shard_map/psum | solution.py:12
  643.9 30.5 %copy-start.11 = (bf16[2048,256]{0,1:T(8,128)(2,1)S(1)}, bf16[2048,256]{0,1:T(8,128)(2,1)}, u32[]{:S(2)}) copy-start(bf16[2048,256]{0,1:T(8,128)(2,1)} %all-reduce.22.cloned.1.call-done) | copy-start | bytes 3145732
  674.4 5.5 copy-start.4
  674.4 5.5 copy-start.5
Sparse Core Ops, SparseCore 0:
  76.4 33.3 all-reduce.29
  115.3 77.8 all-reduce.13
  196.1 31.5 all-reduce.15
  299.9 33.5 all-reduce.27
  338.3 77.7 all-reduce.17
  419.1 31.5 all-reduce.19
  523.6 33.5 all-reduce.25
  562.0 77.8 all-reduce.21
  642.8 31.5 all-reduce.23
where the time goes:
time: 708 us; the launch traced here: 696 us
  waiting for transfers between devices  420 us (59%)
  other arithmetic  182 us (26%)
  local copies, waits for them, and re-layouts  42.3 us (6%)
  matrix products  33.3 us (5%)
  between operations  17.9 us (3%)
    psum x9, waiting for transfers between devices, broadcast(): return lax.psum(kept, axis)  420 us
    another operation x20, other arithmetic, factor_tile(): factor = jnp.linalg.cholesky(square)  104 us
    another operation x4, other arithmetic, factor_tile(): inverse = jax.scipy.linalg.solve_triangular(factor, eye_tile, lower=True)  59.2 us
    unnamed x38, local copies, waits for them, and re-layouts  15.5 us
    dot_general x3, matrix products, on_device(): jnp.dot(column_old, inverse.T, precision=lax.Precision.HIGHEST, preferred...  14.7 us
    dot_general x3, matrix products, tile_product(): lax.dot_general(left_rows, right_rows, (((1,), (1,)), ((), ())), preferre...  14.6 us
  transfers between devices with their start and end apart: 9, of which 9 were waited for; matrix products, arithmetic and copies ran while one was open for 1% of the time, Pallas kernels for 0%

commit v1 on v0

v1 whole, which is shorter than its diff:
```python
import functools

import jax
import jax.numpy as jnp
from jax import lax
from jax.experimental import pallas as pl
from jax.experimental.pallas import tpu as pltpu
from jax.sharding import PartitionSpec as P

TILE = 256
PANELS = 3
SLAB = 32
LANES = 128
MESH = pl.DeviceIdType.MESH


def lane_splat(value, lane):
    return jnp.broadcast_to(value[:, lane : lane + 1], value.shape)


def row_splat(value, row):
    return jnp.broadcast_to(value[row : row + 1, :], value.shape)


def eliminate(tiles):
    row = lax.broadcasted_iota(jnp.int32, tiles[0].shape, 0)
    for j in range(0, SLAB, 2):
        c1, c2 = lane_splat(tiles[0], j), lane_splat(tiles[0], j + 1)
        a, b, d = row_splat(c1, j), row_splat(c1, j + 1), row_splat(c2, j + 1)
        ra = 1.0 / a
        rest = 1.0 / (a * d - b * b)
        ratio = b * ra
        m1 = jnp.where(row > j, c1 * ra, 0.0)
        m2 = jnp.where(row > j + 1, (c2 - c1 * ratio) * (a * rest), 0.0)
        new = []
        for tile in tiles:
            r1 = row_splat(tile, j)
            r2 = row_splat(tile, j + 1) - ratio * r1
            new.append(tile - m1 * r1 - m2 * r2)
        tiles = new
    lane = lax.broadcasted_iota(jnp.int32, tiles[0].shape, 1)
    pivots = jnp.sum(jnp.where(lane == row, tiles[0], 0.0), axis=1, keepdims=True)
    scale = lax.rsqrt(jnp.broadcast_to(pivots, tiles[0].shape))
    return [tile * scale for tile in tiles[1:]]


def down_product(left, right):
    return lax.dot_general(
        left,
        right,
        (((0,), (0,)), ((), ())),
        precision=lax.Precision.HIGHEST,
        preferred_element_type=jnp.float32,
    )


def factor_tile(square, inverse, upper):
    full = (TILE, TILE)
    eye = lax.broadcasted_iota(jnp.int32, full, 0) == lax.broadcasted_iota(jnp.int32, full, 1)
    inverse[...] = jnp.where(eye, 1.0, 0.0)
    for half in range(TILE // LANES):
        base = half * LANES
        width = TILE - base

        def block(index, _, base=base, width=width):
            shift = pl.multiple_of(index * SLAB, SLAB)
            rows = pl.ds(pl.multiple_of(base + shift, SLAB), SLAB)
            slab = [square[rows, s : s + LANES] for s in range(base, TILE, LANES)]
            back = [inverse[rows, s : s + LANES] for s in range(0, base + LANES, LANES)]
            pivot = pltpu.roll(slab[0], lax.rem(LANES - shift, LANES), 1)
            done = eliminate([pivot] + slab + back)
            top = jnp.concatenate(done[: len(slab)], axis=1) if len(slab) > 1 else done[0]
            low = done[len(slab) :]
            low = jnp.concatenate(low, axis=1) if len(low) > 1 else low[0]
            lane = lax.broadcasted_iota(jnp.int32, (SLAB, width), 1)
            row = lax.broadcasted_iota(jnp.int32, (SLAB, width), 0) + shift
            top = jnp.where(lane >= row, top, 0.0)
            after = jnp.where(lane >= shift + SLAB, top, 0.0)
            upper[rows, base:] = top
            if base:
                upper[rows, :base] = jnp.zeros((SLAB, base), jnp.float32)
            inverse[rows, : base + LANES] = low
            square[base:, base:] -= down_product(after, top)
            inverse[base:, : base + LANES] -= down_product(after, low)
            return 0

        lax.fori_loop(0, LANES // SLAB, block, 0)


def kernel(
    row_count,
    col_count,
    matrix,
    out,
    block,
    rounded,
    across,
    inverses,
    square,
    upper,
    load_sem,
    inv_send,
    inv_recv,
    rows_send,
    rows_recv,
    across_send,
    across_recv,
):
    row, col = lax.axis_index("row"), lax.axis_index("col")
    tiles_down = block.shape[0] // TILE
    tiles_across = block.shape[1] // TILE
    load = pltpu.make_async_copy(matrix, block, load_sem)
    load.start()

    barrier = pltpu.get_barrier_semaphore()
    for step in range(1, row_count):
        other = lax.rem(row + step, row_count)
        pl.semaphore_signal(barrier, inc=1, device_id=(other, col), device_id_type=MESH)
    twin = col + 1 - 2 * lax.rem(col, 2)
    pl.semaphore_signal(barrier, inc=1, device_id=(row, twin), device_id_type=MESH)
    has_up = col + 2 < col_count
    has_down = col >= 2

    @pl.when(has_up)
    def _():
        pl.semaphore_signal(barrier, inc=1, device_id=(row, col + 2), device_id_type=MESH)

    @pl.when(has_down)
    def _():
        pl.semaphore_signal(barrier, inc=1, device_id=(row, col - 2), device_id_type=MESH)

    pl.semaphore_wait(barrier, row_count + has_up.astype(jnp.int32) + has_down.astype(jnp.int32))
    load.wait()

    def tile_rows(t):
        return pl.ds(pl.multiple_of(t * TILE, TILE), TILE)

    def inverse_copy(k, step):
        return pltpu.make_async_remote_copy(
            src_ref=inverses.at[k],
            dst_ref=inverses.at[k],
            send_sem=inv_send.at[k, step],
            recv_sem=inv_recv.at[k],
            device_id=(lax.rem(row + step, row_count), col),
            device_id_type=MESH,
        )

    def rows_copy(k, t, way, target):
        return pltpu.make_async_remote_copy(
            src_ref=rounded.at[k, t],
            dst_ref=rounded.at[k, t],
            send_sem=rows_send.at[k, t, way],
            recv_sem=rows_recv.at[k, t],
            device_id=(row, target),
            device_id_type=MESH,
        )

    def across_copy(k, u, step):
        return pltpu.make_async_remote_copy(
            src_ref=rounded.at[k, (u * col_count + col) // row_count],
            dst_ref=across.at[k, u],
            send_sem=across_send.at[k, u, step],
            recv_sem=across_recv.at[k, u],
            device_id=(lax.rem(row + step, row_count), col),
            device_id_type=MESH,
        )

    holds_across = row == lax.rem(col, row_count)

    def sends(k):
        in_lane = lax.rem(col + k, 2) == 0
        up = jnp.logical_and(in_lane, jnp.logical_and(col >= k, has_up))
        down = jnp.logical_and(in_lane, jnp.logical_and(col <= k, has_down))
        return ((in_lane, twin), (up, col + 2), (down, col - 2))

    def pass_on(k, t):
        for way, (do, target) in enumerate(sends(k)):

            @pl.when(do)
            def _(way=way, target=target):
                rows_copy(k, t, way, target).start()

    def send_across(k, u):
        for step in range(1, row_count):
            across_copy(k, u, step).start()

    def update(k, u, t, partner):
        i, j = t * row_count + row, u * col_count + col

        @pl.when(jnp.logical_and(i >= j, j > k))
        def _():
            product = lax.dot_general(
                rounded[k, t],
                partner,
                (((1,), (1,)), ((), ())),
                preferred_element_type=jnp.float32,
            )
            block[tile_rows(t), u * TILE : (u + 1) * TILE] -= product

    def update_column(k, u, first):
        @pl.when(holds_across)
        def _():
            across[k, u] = rounded[k, (u * col_count + col) // row_count]

        @pl.when(jnp.logical_not(holds_across))
        def _():
            across_copy(k, u, 1).wait_recv()

        def one(t, _):
            update(k, u, t, across[k, u])
            return 0

        lax.fori_loop(first, tiles_down, one, 0)

    def panel(k, _):
        last = k - 1
        ahead = jnp.logical_and(row == k, col == k)
        later = jnp.logical_and(ahead, k > 0)

        @pl.when(later)
        def _():
            rows_copy(last, 0, 0, twin).wait_recv()
            send_across(last, 0)
            update(last, 0, 0, rounded[last, 0])

        @pl.when(jnp.logical_and(ahead, k < PANELS))
        def _():
            square[...] = block[0:TILE, 0:TILE]
            factor_tile(square, inverses.at[k], upper)
            for step in range(1, row_count):
                inverse_copy(k, step).start()
            block[0:TILE, 0:TILE] = upper[...].T

        @pl.when(k > 0)
        def _():
            @pl.when(col != last)
            def _():
                def receive(t, _):
                    rows_copy(last, t, 0, twin).wait_recv()
                    pass_on(last, t)
                    return 0

                lax.fori_loop(later.astype(jnp.int32), tiles_down, receive, 0)

            @pl.when(holds_across)
            def _():
                @pl.when(jnp.logical_not(later))
                def _():
                    send_across(last, 0)

                for u in range(1, tiles_across):
                    send_across(last, u)

            update_column(last, 0, later.astype(jnp.int32))

        @pl.when(jnp.logical_and(col == k, k < PANELS))
        def _():
            @pl.when(row != k)
            def _():
                inverse_copy(k, 1).wait_recv()

            def solve(t, _):
                below = t * row_count + row > k

                @pl.when(below)
                def _():
                    solved = lax.dot_general(
                        block[tile_rows(t), 0:TILE],
                        inverses[k],
                        (((1,), (1,)), ((), ())),
                        precision=lax.Precision.HIGHEST,
                        preferred_element_type=jnp.float32,
                    )
                    block[tile_rows(t), 0:TILE] = solved
                    rounded[k, t] = solved.astype(jnp.bfloat16)

                @pl.when(jnp.logical_not(below))
                def _():
                    rounded[k, t] = jnp.zeros((TILE, TILE), jnp.bfloat16)

                pass_on(k, t)
                return 0

            lax.fori_loop(0, tiles_down, solve, 0)

        @pl.when(k > 0)
        def _():
            for u in range(1, tiles_across):
                update_column(last, u, 0)

        return 0

    lax.fori_loop(0, PANELS + 1, panel, 0)

    store = pltpu.make_async_copy(block, out, load_sem)
    store.start()

    def finish(k, _):
        @pl.when(jnp.logical_and(row == k, col == k))
        def _():
            for step in range(1, row_count):
                inverse_copy(k, step).wait_send()

        def rows_done(t, _):
            for way, (do, target) in enumerate(sends(k)):

                @pl.when(do)
                def _(way=way, target=target):
                    rows_copy(k, t, way, target).wait_send()

            return 0

        lax.fori_loop(0, tiles_down, rows_done, 0)

        @pl.when(holds_across)
        def _():
            for u in range(tiles_across):
                for step in range(1, row_count):
                    across_copy(k, u, step).wait_send()

        return 0

    lax.fori_loop(0, PANELS, finish, 0)
    store.wait()


def on_device(row_count, col_count, matrix):
    tiles_down = matrix.shape[0] // TILE
    tiles_across = matrix.shape[1] // TILE
    square = (TILE, TILE)
    return pl.pallas_call(
        functools.partial(kernel, row_count, col_count),
        out_shape=jax.ShapeDtypeStruct(matrix.shape, jnp.float32),
        in_specs=[pl.BlockSpec(memory_space=pl.ANY)],
        out_specs=pl.BlockSpec(memory_space=pl.ANY),
        scratch_shapes=[
            pltpu.VMEM(matrix.shape, jnp.float32),
            pltpu.VMEM((PANELS, tiles_down) + square, jnp.bfloat16),
            pltpu.VMEM((PANELS, tiles_across) + square, jnp.bfloat16),
            pltpu.VMEM((PANELS,) + square, jnp.float32),
            pltpu.VMEM(square, jnp.float32),
            pltpu.VMEM(square, jnp.float32),
            pltpu.SemaphoreType.DMA,
            pltpu.SemaphoreType.DMA((PANELS, row_count)),
            pltpu.SemaphoreType.DMA((PANELS,)),
            pltpu.SemaphoreType.DMA((PANELS, tiles_down, 3)),
            pltpu.SemaphoreType.DMA((PANELS, tiles_down)),
            pltpu.SemaphoreType.DMA((PANELS, tiles_across, row_count)),
            pltpu.SemaphoreType.DMA((PANELS, tiles_across)),
        ],
        compiler_params=pltpu.CompilerParams(
            collective_id=0, has_side_effects=True, vmem_limit_bytes=40 * 1024 * 1024
        ),
        name="panels",
    )(matrix)


def solution(mesh):
    return jax.shard_map(
        functools.partial(on_device, mesh.shape["row"], mesh.shape["col"]),
        mesh=mesh,
        in_specs=(P("row", "col"),),
        out_specs=P("row", "col"),
        check_vma=False,
    )
```

time: 708 us -> 145 us (0.20)
  the two profiles are of different devices: /device:TPU:26 before, /device:TPU:29 now
where the time goes in v1:
time: 145 us
  Pallas kernels  141 us (97%)
  local copies, waits for them, and re-layouts  4.2 us (3%)
    pallas_call x1, Pallas kernels, on_device(): pl.pallas_call(functools.partial(kernel, row_count, col_count), out_shape...  141 us
    unnamed x3, local copies, waits for them, and re-layouts  4.2 us

profile of v1, /device:TPU:29, one launch (start us, length us, event | category | flops | bytes accessed | tf_op | source)
XLA Modules:
  0.0 145.3 jit_solution(5577530727802530039)
XLA Ops:
  0.0 0.0 copy-start
  0.0 2.2 %copy-done = f32[2048,512]{1,0:T(8,128)S(1)} copy-done((f32[2048,512]{1,0:T(8,128)S(1)}, f32[2048,512]{1,0:T(8,128)}, u32[]{:S(2)}) %copy-start) | copy-done | bytes 4194328
  2.2 141.1 %panels.1 = f32[2048,512]{1,0:T(8,128)S(1)} custom-call(f32[2048,512]{1,0:T(8,128)S(1)} %copy-done), custom_call_target="tpu_custom_call" | custom-call | tf_op jit(solution)/shard_map/panels/pallas_call | solution.py:331
  143.3 2.0 %copy.3 = f32[2048,512]{1,0:T(8,128)} copy(f32[2048,512]{1,0:T(8,128)S(1)} %panels.1) | data formatting | bytes 8388608
Async XLA Ops:
  0.0 2.2 %copy-start = (f32[2048,512]{1,0:T(8,128)S(1)}, f32[2048,512]{1,0:T(8,128)}, u32[]{:S(2)}) copy-start(f32[2048,512]{1,0:T(8,128)} %matrix.1) | copy-start | bytes 12582916

commit v2 on v1

--- a/solution.py
+++ b/solution.py
@@ -10,6 +10,7 @@
 TILE = 256
 PANELS = 3
 SLAB = 32
+GROUP = 8
 LANES = 128
 MESH = pl.DeviceIdType.MESH
 
@@ -23,32 +24,43 @@
 
 
 def eliminate(tiles):
+    finished = [[] for _ in tiles]
+    for start in range(0, SLAB, GROUP):
+        columns = [lane_splat(tiles[0], start + q) for q in range(GROUP)]
+        row = lax.broadcasted_iota(jnp.int32, tiles[0].shape, 0)
+        for j in range(0, GROUP, 2):
+            c1, c2 = columns[j], columns[j + 1]
+            a, b, d = row_splat(c1, j), row_splat(c1, j + 1), row_splat(c2, j + 1)
+            ra = 1.0 / a
+            rest = a / (a * d - b * b)
+            ratio = b * ra
+            m1 = jnp.where(row > j, c1 * ra, 0.0)
+            m2 = jnp.where(row > j + 1, (c2 - c1 * ratio) * rest, 0.0)
+            for q in range(j + 2, GROUP):
+                x1 = row_splat(c1, q)
+                x2 = row_splat(c2, q) - ratio * x1
+                columns[q] = columns[q] - m1 * x1 - m2 * x2
+            new = []
+            for tile in tiles:
+                r1 = row_splat(tile, j)
+                r2 = row_splat(tile, j + 1) - ratio * r1
+                new.append(tile - m1 * r1 - m2 * r2)
+            tiles = new
+        for kept, tile in zip(finished, tiles):
+            kept.append(tile[:GROUP])
+        tiles = [tile[GROUP:] for tile in tiles]
+    tiles = [jnp.concatenate(kept, axis=0) for kept in finished]
     row = lax.broadcasted_iota(jnp.int32, tiles[0].shape, 0)
-    for j in range(0, SLAB, 2):
-        c1, c2 = lane_splat(tiles[0], j), lane_splat(tiles[0], j + 1)
-        a, b, d = row_splat(c1, j), row_splat(c1, j + 1), row_splat(c2, j + 1)
-        ra = 1.0 / a
-        rest = 1.0 / (a * d - b * b)
-        ratio = b * ra
-        m1 = jnp.where(row > j, c1 * ra, 0.0)
-        m2 = jnp.where(row > j + 1, (c2 - c1 * ratio) * (a * rest), 0.0)
-        new = []
-        for tile in tiles:
-            r1 = row_splat(tile, j)
-            r2 = row_splat(tile, j + 1) - ratio * r1
-            new.append(tile - m1 * r1 - m2 * r2)
-        tiles = new
     lane = lax.broadcasted_iota(jnp.int32, tiles[0].shape, 1)
     pivots = jnp.sum(jnp.where(lane == row, tiles[0], 0.0), axis=1, keepdims=True)
     scale = lax.rsqrt(jnp.broadcast_to(pivots, tiles[0].shape))
     return [tile * scale for tile in tiles[1:]]
 
 
-def down_product(left, right):
-    return lax.dot_general(
+def precise_product(left, right):
+    return jnp.dot(
         left,
         right,
-        (((0,), (0,)), ((), ())),
         precision=lax.Precision.HIGHEST,
         preferred_element_type=jnp.float32,
     )
@@ -58,33 +70,30 @@
     full = (TILE, TILE)
     eye = lax.broadcasted_iota(jnp.int32, full, 0) == lax.broadcasted_iota(jnp.int32, full, 1)
     inverse[...] = jnp.where(eye, 1.0, 0.0)
-    for half in range(TILE // LANES):
-        base = half * LANES
-        width = TILE - base
-
-        def block(index, _, base=base, width=width):
-            shift = pl.multiple_of(index * SLAB, SLAB)
-            rows = pl.ds(pl.multiple_of(base + shift, SLAB), SLAB)
-            slab = [square[rows, s : s + LANES] for s in range(base, TILE, LANES)]
-            back = [inverse[rows, s : s + LANES] for s in range(0, base + LANES, LANES)]
-            pivot = pltpu.roll(slab[0], lax.rem(LANES - shift, LANES), 1)
-            done = eliminate([pivot] + slab + back)
-            top = jnp.concatenate(done[: len(slab)], axis=1) if len(slab) > 1 else done[0]
-            low = done[len(slab) :]
-            low = jnp.concatenate(low, axis=1) if len(low) > 1 else low[0]
-            lane = lax.broadcasted_iota(jnp.int32, (SLAB, width), 1)
-            row = lax.broadcasted_iota(jnp.int32, (SLAB, width), 0) + shift
-            top = jnp.where(lane >= row, top, 0.0)
-            after = jnp.where(lane >= shift + SLAB, top, 0.0)
-            upper[rows, base:] = top
-            if base:
-                upper[rows, :base] = jnp.zeros((SLAB, base), jnp.float32)
-            inverse[rows, : base + LANES] = low
-            square[base:, base:] -= down_product(after, top)
-            inverse[base:, : base + LANES] -= down_product(after, low)
-            return 0
-
-        lax.fori_loop(0, LANES // SLAB, block, 0)
+    upper[...] = jnp.zeros(full, jnp.float32)
+    for first in range(0, TILE, SLAB):
+        base = first // LANES * LANES
+        reach = base + LANES
+        shift = first - base
+        rows = slice(first, first + SLAB)
+        slab = [square[rows, s : s + LANES] for s in range(base, TILE, LANES)]
+        back = [inverse[rows, s : s + LANES] for s in range(0, reach, LANES)]
+        pivot = pltpu.roll(slab[0], LANES - shift, 1) if shift else slab[0]
+        done = eliminate([pivot] + slab + back)
+        top = jnp.concatenate(done[: len(slab)], axis=1) if len(slab) > 1 else done[0]
+        low = done[len(slab) :]
+        low = jnp.concatenate(low, axis=1) if len(low) > 1 else low[0]
+        lane = lax.broadcasted_iota(jnp.int32, top.shape, 1)
+        row = lax.broadcasted_iota(jnp.int32, top.shape, 0) + shift
+        top = jnp.where(lane >= row, top, 0.0)
+        upper[rows, base:] = top
+        inverse[rows, :reach] = low
+        flipped = top.T
+        for near, far in ((first + SLAB, first + 2 * SLAB), (first + 2 * SLAB, TILE)):
+            if near < far <= TILE:
+                left = flipped[near - base : far - base]
+                square[near:far, base:] -= precise_product(left, top)
+                inverse[near:far, :reach] -= precise_product(left, low)
 
 
 def kernel(
@@ -167,14 +176,21 @@
 
     holds_across = row == lax.rem(col, row_count)
 
-    def sends(k):
-        in_lane = lax.rem(col + k, 2) == 0
-        up = jnp.logical_and(in_lane, jnp.logical_and(col >= k, has_up))
-        down = jnp.logical_and(in_lane, jnp.logical_and(col <= k, has_down))
-        return ((in_lane, twin), (up, col + 2), (down, col - 2))
+    def sends(k, t):
+        split = k == PANELS - 1
+        odd = jnp.where(split, lax.rem(t, 2), 0)
+        in_lane = lax.rem(col + k + odd, 2) == 0
+        own_twin = k + 1 - 2 * lax.rem(k, 2)
+        place, source = col // 2, k // 2
+        up = jnp.logical_and(in_lane, jnp.logical_and(place >= source, has_up))
+        down = jnp.logical_and(in_lane, jnp.logical_and(place <= source, has_down))
+        returns = jnp.logical_and(split, jnp.logical_and(odd == 0, col == own_twin + 2))
+        first = jnp.logical_and(col == k, jnp.logical_or(jnp.logical_not(split), odd == 1))
+        cross = jnp.logical_or(first, jnp.logical_and(in_lane, place != source))
+        return ((cross, twin), (up, col + 2), (jnp.logical_or(down, returns), col - 2))
 
     def pass_on(k, t):
-        for way, (do, target) in enumerate(sends(k)):
+        for way, (do, target) in enumerate(sends(k, t)):
 
             @pl.when(do)
             def _(way=way, target=target):
@@ -302,7 +318,7 @@
                 inverse_copy(k, step).wait_send()
 
         def rows_done(t, _):
-            for way, (do, target) in enumerate(sends(k)):
+            for way, (do, target) in enumerate(sends(k, t)):
 
                 @pl.when(do)
                 def _(way=way, target=target):
@@ -349,7 +365,7 @@
             pltpu.SemaphoreType.DMA((PANELS, tiles_across)),
         ],
         compiler_params=pltpu.CompilerParams(
-            collective_id=0, has_side_effects=True, vmem_limit_bytes=40 * 1024 * 1024
+            collective_id=0, has_side_effects=True, vmem_limit_bytes=60 * 1024 * 1024
         ),
         name="panels",
     )(matrix)

time: 145 us -> 177 us (1.22)
  the two profiles are of different devices: /device:TPU:29 before, /device:TPU:25 now
where the time goes in v2:
time: 177 us
  Pallas kernels  172 us (97%)
  local copies, waits for them, and re-layouts  4.64 us (3%)
    pallas_call x1, Pallas kernels, on_device(): pl.pallas_call(functools.partial(kernel, row_count, col_count), out_shape...  172 us
    unnamed x1, local copies, waits for them, and re-layouts  4.64 us

profile of v2, /device:TPU:25, one launch (start us, length us, event | category | flops | bytes accessed | tf_op | source)
XLA Modules:
  0.0 176.7 jit_solution(2194842257399046803)
XLA Ops:
  0.0 172.0 %panels.1 = f32[2048,512]{1,0:T(8,128)} custom-call(f32[2048,512]{1,0:T(8,128)} %matrix.1), custom_call_target="tpu_custom_call" | custom-call | tf_op jit(solution)/shard_map/panels/pallas_call | solution.py:347
  172.0 4.6 %copy.3 = f32[2048,512]{1,0:T(8,128)} copy(f32[2048,512]{1,0:T(8,128)} %panels.1) | data formatting | bytes 8388608

commit v3 on v2

--- a/solution.py
+++ b/solution.py
@@ -164,9 +164,12 @@
             device_id_type=MESH,
         )
 
+    def across_row(u):
+        return (u * col_count + col) // row_count
+
     def across_copy(k, u, step):
         return pltpu.make_async_remote_copy(
-            src_ref=rounded.at[k, (u * col_count + col) // row_count],
+            src_ref=rounded.at[k, across_row(u)],
             dst_ref=across.at[k, u],
             send_sem=across_send.at[k, u, step],
             recv_sem=across_recv.at[k, u],
@@ -189,6 +192,16 @@
         cross = jnp.logical_or(first, jnp.logical_and(in_lane, place != source))
         return ((cross, twin), (up, col + 2), (jnp.logical_or(down, returns), col - 2))
 
+    def arrival(k, step):
+        own = lax.rem(col + k, 2)
+        end = step == tiles_down - 1
+        ahead = jnp.logical_or(step == 0, jnp.logical_and(lax.rem(step, 2) == 1, step < tiles_down - 1))
+        place = jnp.where(
+            ahead, (step + 1) // 2, jnp.where(end, tiles_down // 2 - 1, (step + tiles_down - 2) // 2 - tiles_down // 2)
+        )
+        mixed = 2 * place + jnp.where(ahead, own, 1 - own)
+        return jnp.where(k == PANELS - 1, mixed, step)
+
     def pass_on(k, t):
         for way, (do, target) in enumerate(sends(k, t)):
 
@@ -216,7 +229,7 @@
     def update_column(k, u, first):
         @pl.when(holds_across)
         def _():
-            across[k, u] = rounded[k, (u * col_count + col) // row_count]
+            across[k, u] = rounded[k, across_row(u)]
 
         @pl.when(jnp.logical_not(holds_across))
         def _():
@@ -230,7 +243,7 @@
 
     def panel(k, _):
         last = k - 1
-        ahead = jnp.logical_and(row == k, col == k)
+        ahead = jnp.logical_and(k < PANELS, jnp.logical_and(row == k, col == k))
         later = jnp.logical_and(ahead, k > 0)
 
         @pl.when(later)
@@ -239,7 +252,7 @@
             send_across(last, 0)
             update(last, 0, 0, rounded[last, 0])
 
-        @pl.when(jnp.logical_and(ahead, k < PANELS))
+        @pl.when(ahead)
         def _():
             square[...] = block[0:TILE, 0:TILE]
             factor_tile(square, inverses.at[k], upper)
@@ -251,20 +264,23 @@
         def _():
             @pl.when(col != last)
             def _():
-                def receive(t, _):
+                def receive(step, _):
+                    t = arrival(last, step)
                     rows_copy(last, t, 0, twin).wait_recv()
                     pass_on(last, t)
+                    for u in range(tiles_across):
+
+                        @pl.when(jnp.logical_and(holds_across, t == across_row(u)))
+                        def _(u=u):
+                            send_across(last, u)
+
                     return 0
 
                 lax.fori_loop(later.astype(jnp.int32), tiles_down, receive, 0)
 
-            @pl.when(holds_across)
+            @pl.when(jnp.logical_and(col == last, holds_across))
             def _():
-                @pl.when(jnp.logical_not(later))
-                def _():
-                    send_across(last, 0)
-
-                for u in range(1, tiles_across):
+                for u in range(tiles_across):
                     send_across(last, u)
 
             update_column(last, 0, later.astype(jnp.int32))
@@ -365,7 +381,7 @@
             pltpu.SemaphoreType.DMA((PANELS, tiles_across)),
         ],
         compiler_params=pltpu.CompilerParams(
-            collective_id=0, has_side_effects=True, vmem_limit_bytes=60 * 1024 * 1024
+            collective_id=0, has_side_effects=True, vmem_limit_bytes=40 * 1024 * 1024
         ),
         name="panels",
     )(matrix)

time: 177 us -> 119 us (0.67)
  the two profiles are of different devices: /device:TPU:25 before, /device:TPU:26 now
where the time goes in v3:
time: 119 us
  Pallas kernels  115 us (97%)
  local copies, waits for them, and re-layouts  4.2 us (4%)
    pallas_call x1, Pallas kernels, on_device(): pl.pallas_call(functools.partial(kernel, row_count, col_count), out_shape...  115 us
    unnamed x3, local copies, waits for them, and re-layouts  4.2 us

profile of v3, /device:TPU:26, one launch (start us, length us, event | category | flops | bytes accessed | tf_op | source)
XLA Modules:
  0.0 118.9 jit_solution(10690318914173288442)
XLA Ops:
  0.0 0.0 copy-start
  0.0 2.2 %copy-done = f32[2048,512]{1,0:T(8,128)S(1)} copy-done((f32[2048,512]{1,0:T(8,128)S(1)}, f32[2048,512]{1,0:T(8,128)}, u32[]{:S(2)}) %copy-start) | copy-done | bytes 4194328
  2.2 114.7 %panels.1 = f32[2048,512]{1,0:T(8,128)S(1)} custom-call(f32[2048,512]{1,0:T(8,128)S(1)} %copy-done), custom_call_target="tpu_custom_call" | custom-call | tf_op jit(solution)/shard_map/panels/pallas_call | solution.py:363
  116.9 2.0 %copy.3 = f32[2048,512]{1,0:T(8,128)} copy(f32[2048,512]{1,0:T(8,128)S(1)} %panels.1) | data formatting | bytes 8388608
Async XLA Ops:
  0.0 2.2 %copy-start = (f32[2048,512]{1,0:T(8,128)S(1)}, f32[2048,512]{1,0:T(8,128)}, u32[]{:S(2)}) copy-start(f32[2048,512]{1,0:T(8,128)} %matrix.1) | copy-start | bytes 12582916

commit v4 on v3

--- a/solution.py
+++ b/solution.py
@@ -9,7 +9,7 @@
 
 TILE = 256
 PANELS = 3
-SLAB = 32
+SLAB = 64
 GROUP = 8
 LANES = 128
 MESH = pl.DeviceIdType.MESH

time: 119 us -> 118 us (level)
  no operation moved by 1% of the time
where the time goes in v4:
time: 118 us
  Pallas kernels  114 us (97%)
  local copies, waits for them, and re-layouts  4.2 us (4%)
    pallas_call x1, Pallas kernels, on_device(): pl.pallas_call(functools.partial(kernel, row_count, col_count), out_shape...  114 us
    unnamed x3, local copies, waits for them, and re-layouts  4.2 us

profile of v4, /device:TPU:26, one launch (start us, length us, event | category | flops | bytes accessed | tf_op | source)
XLA Modules:
  0.0 118.0 jit_solution(16833756999817820127)
XLA Ops:
  0.0 0.0 copy-start
  0.0 2.2 %copy-done = f32[2048,512]{1,0:T(8,128)S(1)} copy-done((f32[2048,512]{1,0:T(8,128)S(1)}, f32[2048,512]{1,0:T(8,128)}, u32[]{:S(2)}) %copy-start) | copy-done | bytes 4194328
  2.2 113.8 %panels.1 = f32[2048,512]{1,0:T(8,128)S(1)} custom-call(f32[2048,512]{1,0:T(8,128)S(1)} %copy-done), custom_call_target="tpu_custom_call" | custom-call | tf_op jit(solution)/shard_map/panels/pallas_call | solution.py:363
  116.0 2.0 %copy.3 = f32[2048,512]{1,0:T(8,128)} copy(f32[2048,512]{1,0:T(8,128)S(1)} %panels.1) | data formatting | bytes 8388608
Async XLA Ops:
  0.0 2.2 %copy-start = (f32[2048,512]{1,0:T(8,128)S(1)}, f32[2048,512]{1,0:T(8,128)}, u32[]{:S(2)}) copy-start(f32[2048,512]{1,0:T(8,128)} %matrix.1) | copy-start | bytes 12582916

commit v5 on v4

--- a/solution.py
+++ b/solution.py
@@ -179,6 +179,9 @@
 
     holds_across = row == lax.rem(col, row_count)
 
+    def live(k, t):
+        return t * row_count + row > k
+
     def sends(k, t):
         split = k == PANELS - 1
         odd = jnp.where(split, lax.rem(t, 2), 0)
@@ -190,7 +193,8 @@
         returns = jnp.logical_and(split, jnp.logical_and(odd == 0, col == own_twin + 2))
         first = jnp.logical_and(col == k, jnp.logical_or(jnp.logical_not(split), odd == 1))
         cross = jnp.logical_or(first, jnp.logical_and(in_lane, place != source))
-        return ((cross, twin), (up, col + 2), (jnp.logical_or(down, returns), col - 2))
+        ways = ((cross, twin), (up, col + 2), (jnp.logical_or(down, returns), col - 2))
+        return tuple((jnp.logical_and(live(k, t), do), target) for do, target in ways)
 
     def arrival(k, step):
         own = lax.rem(col + k, 2)
@@ -266,7 +270,15 @@
             def _():
                 def receive(step, _):
                     t = arrival(last, step)
-                    rows_copy(last, t, 0, twin).wait_recv()
+
+                    @pl.when(live(last, t))
+                    def _():
+                        rows_copy(last, t, 0, twin).wait_recv()
+
+                    @pl.when(jnp.logical_not(live(last, t)))
+                    def _():
+                        rounded[last, t] = jnp.zeros((TILE, TILE), jnp.bfloat16)
+
                     pass_on(last, t)
                     for u in range(tiles_across):
 

time: 118 us -> 112 us (0.949); the launches traced: 118 us -> 110 us
  Pallas kernels: 114 us -> 106 us
    pallas_call x1, Pallas kernels: 114 us -> 106 us  [on_device(): pl.pallas_call(functools.partial(kernel, row_count, col_count), out_shape...]
where the time goes in v5:
time: 112 us; the launch traced here: 110 us
  Pallas kernels  106 us (95%)
  local copies, waits for them, and re-layouts  4.2 us (4%)
    pallas_call x1, Pallas kernels, on_device(): pl.pallas_call(functools.partial(kernel, row_count, col_count), out_shape...  106 us
    unnamed x3, local copies, waits for them, and re-layouts  4.2 us

profile of v5, /device:TPU:26, one launch (start us, length us, event | category | flops | bytes accessed | tf_op | source)
XLA Modules:
  0.0 110.2 jit_solution(8951062614033447810)
XLA Ops:
  0.0 0.0 copy-start
  0.0 2.2 %copy-done = f32[2048,512]{1,0:T(8,128)S(1)} copy-done((f32[2048,512]{1,0:T(8,128)S(1)}, f32[2048,512]{1,0:T(8,128)}, u32[]{:S(2)}) %copy-start) | copy-done | bytes 4194328
  2.2 106.0 %panels.1 = f32[2048,512]{1,0:T(8,128)S(1)} custom-call(f32[2048,512]{1,0:T(8,128)S(1)} %copy-done), custom_call_target="tpu_custom_call" | custom-call | tf_op jit(solution)/shard_map/panels/pallas_call | solution.py:375
  108.2 2.0 %copy.3 = f32[2048,512]{1,0:T(8,128)} copy(f32[2048,512]{1,0:T(8,128)S(1)} %panels.1) | data formatting | bytes 8388608
Async XLA Ops:
  0.0 2.2 %copy-start = (f32[2048,512]{1,0:T(8,128)S(1)}, f32[2048,512]{1,0:T(8,128)}, u32[]{:S(2)}) copy-start(f32[2048,512]{1,0:T(8,128)} %matrix.1) | copy-start | bytes 12582916

commit v6 on v5

--- a/solution.py
+++ b/solution.py
@@ -10,7 +10,7 @@
 TILE = 256
 PANELS = 3
 SLAB = 64
-GROUP = 8
+GROUP = 16
 LANES = 128
 MESH = pl.DeviceIdType.MESH
 

time: 112 us -> 111 us (level)
  no operation moved by 1% of the time
where the time goes in v6:
time: 111 us; the launch traced here: 109 us
  Pallas kernels  105 us (95%)
  local copies, waits for them, and re-layouts  4.2 us (4%)
    pallas_call x1, Pallas kernels, on_device(): pl.pallas_call(functools.partial(kernel, row_count, col_count), out_shape...  105 us
    unnamed x3, local copies, waits for them, and re-layouts  4.2 us

profile of v6, /device:TPU:26, one launch (start us, length us, event | category | flops | bytes accessed | tf_op | source)
XLA Modules:
  0.0 109.2 jit_solution(12097046324807185996)
XLA Ops:
  0.0 0.0 copy-start
  0.0 2.2 %copy-done = f32[2048,512]{1,0:T(8,128)S(1)} copy-done((f32[2048,512]{1,0:T(8,128)S(1)}, f32[2048,512]{1,0:T(8,128)}, u32[]{:S(2)}) %copy-start) | copy-done | bytes 4194328
  2.2 104.9 %panels.1 = f32[2048,512]{1,0:T(8,128)S(1)} custom-call(f32[2048,512]{1,0:T(8,128)S(1)} %copy-done), custom_call_target="tpu_custom_call" | custom-call | tf_op jit(solution)/shard_map/panels/pallas_call | solution.py:375
  107.1 2.0 %copy.3 = f32[2048,512]{1,0:T(8,128)} copy(f32[2048,512]{1,0:T(8,128)S(1)} %panels.1) | data formatting | bytes 8388608
Async XLA Ops:
  0.0 2.2 %copy-start = (f32[2048,512]{1,0:T(8,128)S(1)}, f32[2048,512]{1,0:T(8,128)}, u32[]{:S(2)}) copy-start(f32[2048,512]{1,0:T(8,128)} %matrix.1) | copy-start | bytes 12582916
